TPU v7x, 32 devices: a whole 2x2x4 slice. The times are simulated.
32 devices in a mesh: tile: 8 (over y, x, core), expo: 4 (over z).
Axes of the slice: x: 2, y: 2, z: 4, core: 2. Of those that a mesh axis runs over, the one named last changes fastest.
Arguments:
- model: bfloat16 [8, 6, 256, 256], P('tile'), may hold values from -6 to 6
- exp_tile: int32 [1536, 1], P(('tile', 'expo')), may hold values from 0 to 7; in each aligned block of 48 rows (0 to 47, 48 to 95, ...) at most 9 rows name the same one
- exp_band: int32 [1536], P(('tile', 'expo')), may hold values from 0 to 5
- exp_offset: int32 [1536, 2], P(('tile', 'expo')), may hold values from 0 to 64
- pixels: bfloat16 [1536, 128, 128], P(('tile', 'expo')), may hold values from -6 to 6
- inv_var: bfloat16 [1536, 128, 128], P(('tile', 'expo')), may hold values from 0.19921875 to 5
- row_op: bfloat16 [6, 128, 192], replicated, may hold values from -0.4375 to 0.4375
- col_op: bfloat16 [6, 128, 192], replicated, may hold values from -0.4375 to 0.4375
Outputs:
- gradient: float32 [8, 6, 256, 256], P('tile', None, 'expo')
Inputs may be any that keep to these rules, and one draw needn't show every extreme that they name: `exp_tile`: among the 48 cutouts of one device no tile is named more than 9 times, some tile exactly 9 times; every tile is named by some cutout.
All inputs are finite; a program needn't handle non-finite values.
Results may differ from a plain program's by a relative error of at most 0.0027.
Values may be sent and summed in bfloat16 or wider, within the bound.
A program may use at most 64 MiB of HBM per device.

v0:
```python
import math

import jax
import jax.numpy as jnp
from jax import lax
from jax.sharding import PartitionSpec as P

Q = 192


def slot_layout(exp_tile, exp_band, exp_offset, owners, capacity):
    target = exp_tile[:, 0]
    count = target.shape[0]
    order = jnp.arange(count, dtype=jnp.int32)
    before = (target[:, None] == target[None, :]) & (order[None, :] < order[:, None])
    rank = jnp.sum(before.astype(jnp.int32), axis=1)
    slot = target * capacity + rank
    fields = jnp.stack(
        [jnp.ones_like(target), exp_band, exp_offset[:, 0], exp_offset[:, 1]], axis=1
    )
    slot_ids = jnp.arange(owners * capacity, dtype=jnp.int32)
    slot_hot = (slot[:, None] == slot_ids[None, :]).astype(jnp.int32)
    requests = jnp.sum(slot_hot[:, :, None] * fields[:, None, :], axis=0)
    return (slot_hot.astype(jnp.bfloat16), requests)


def to_slots(slot_hot, values):
    return jnp.einsum("ns,nqk->sqk", slot_hot, values, preferred_element_type=jnp.float32).astype(
        jnp.bfloat16
    )


def from_slots(slot_hot, values):
    return jnp.einsum("ns,sqk->nqk", slot_hot, values, preferred_element_type=jnp.float32).astype(
        jnp.bfloat16
    )


def cut_windows(tile_image, requests):

    def one_window(entry):
        return lax.dynamic_slice(tile_image, (entry[1], entry[2], entry[3]), (1, Q, Q))[0]

    windows = jax.vmap(one_window)(requests)
    return windows * requests[:, 0][:, None, None].astype(jnp.bfloat16)


def adjoint_windows(windows, bands, pixels, inv_var, row_op, col_op):
    rows = row_op[bands]
    cols = col_op[bands]
    half = jnp.einsum("nmq,nqk->nmk", rows, windows, preferred_element_type=jnp.float32).astype(
        jnp.bfloat16
    )
    predicted = jnp.einsum("nmk,nlk->nml", half, cols, preferred_element_type=jnp.float32)
    weighted = (inv_var.astype(jnp.float32) * (predicted - pixels.astype(jnp.float32))).astype(
        jnp.bfloat16
    )
    back = jnp.einsum("nmq,nml->nql", rows, weighted, preferred_element_type=jnp.float32).astype(
        jnp.bfloat16
    )
    return jnp.einsum("nql,nlk->nqk", back, cols, preferred_element_type=jnp.float32).astype(
        jnp.bfloat16
    )


def place_windows(total, requests, adjoint):
    bands_n, side, _ = total.shape
    slots = requests.shape[0]
    group = math.gcd(slots, 8)
    inner = jnp.arange(Q, dtype=jnp.int32)
    across = jnp.arange(side, dtype=jnp.int32)
    band_ids = jnp.arange(bands_n, dtype=jnp.int32)

    def step(acc, items):
        entries, pieces = items
        col_hot = (
            across[None, None, :] == entries[:, 3][:, None, None] + inner[None, :, None]
        ).astype(jnp.bfloat16)
        wide = jnp.einsum(
            "nqk,nkp->nqp", pieces, col_hot, preferred_element_type=jnp.float32
        ).astype(jnp.bfloat16)
        row_hot = (
            across[None, :, None] == entries[:, 2][:, None, None] + inner[None, None, :]
        ).astype(jnp.bfloat16)
        placed = jnp.einsum("npq,nqk->npk", row_hot, wide, preferred_element_type=jnp.float32)
        band_hot = (entries[:, 1][:, None] == band_ids[None, :]).astype(jnp.float32) * entries[
            :, 0
        ][:, None].astype(jnp.float32)
        added = jnp.einsum("nb,npk->bpk", band_hot, placed, precision=lax.Precision.HIGHEST)
        return (acc + added, None)

    blocked_req = requests.reshape(slots // group, group, 4)
    blocked_adj = adjoint.reshape(slots // group, group, Q, Q)
    result, _ = lax.scan(step, total, (blocked_req, blocked_adj))
    return result


def local(model, exp_tile, exp_band, exp_offset, pixels, inv_var, row_op, col_op):
    owners = lax.axis_size("tile")
    count = pixels.shape[0]
    capacity = max(2, 3 * count // (2 * owners))
    slot_hot, requests = slot_layout(exp_tile, exp_band, exp_offset, owners, capacity)
    tile_image = model[0]
    partial_value = jnp.zeros(tile_image.shape, jnp.float32)
    received = lax.all_to_all(requests, "tile", split_axis=0, concat_axis=0, tiled=True)
    outgoing = cut_windows(tile_image, received)
    arrived = lax.all_to_all(outgoing, "tile", split_axis=0, concat_axis=0, tiled=True)
    mine = from_slots(slot_hot, arrived)
    adjoint = adjoint_windows(mine, exp_band, pixels, inv_var, row_op, col_op)
    adjoint_slots = to_slots(slot_hot, adjoint)
    returned = lax.all_to_all(adjoint_slots, "tile", split_axis=0, concat_axis=0, tiled=True)
    partial_value = place_windows(partial_value, received, returned)
    summed = lax.psum_scatter(partial_value[None], "expo", scatter_dimension=2, tiled=True)
    return summed


def solution(mesh):
    in_specs = (
        P("tile", None, None, None),
        P(("tile", "expo"), None),
        P(("tile", "expo")),
        P(("tile", "expo"), None),
        P(("tile", "expo"), None, None),
        P(("tile", "expo"), None, None),
        P(),
        P(),
    )
    out_specs = P("tile", None, "expo", None)
    return jax.shard_map(local, mesh=mesh, in_specs=in_specs, out_specs=out_specs, check_vma=False)
```

profile of v0, /device:TPU:0, one launch (start us, length us, event | category | flops | bytes accessed | tf_op | source)
XLA Modules:
  0.0 658.5 jit_solution(8895796802935434118)
XLA Ops:
  9.8 5.2 all-to-all-start
  14.9 4.8 all-to-all-done
  19.8 306.9 %while.13 = (s32[]{:T(128)}, bf16[6,256,256]{2,1,0:T(8,128)(2,1)}, s32[72,3]{0,1:T(4,128)S(1)}, bf16[72,1,192,192]{3,2,1,0:T(8,128)(2,1)}, s32[]{:T(128)}) while((s32[]{:T(128)}, bf16[6,256,256]{2,1,0:T(8,128)(2,1)}, s32[72,3]{0,1:T(4,128)S(1)}, bf16[72,1,192,192]{3,2,1,0:T(8,128)(2,1)}, s32[]{:T(128)}) %tuple.64), condition=%wide.while_cond, body=%wide.while_body.sunk | while | flops 2 | bytes 198769 | solution.py:42
  33.3 3.6 bitcast_dynamic-update-slice_fusion.2
  54.6 3.6 bitcast_dynamic-update-slice_fusion.2
  71.6 3.6 bitcast_dynamic-update-slice_fusion.2
  75.9 3.6 bitcast_dynamic-update-slice_fusion.2
  88.7 3.6 bitcast_dynamic-update-slice_fusion.2
  97.2 3.6 bitcast_dynamic-update-slice_fusion.2
  105.7 3.6 bitcast_dynamic-update-slice_fusion.2
  122.8 3.6 bitcast_dynamic-update-slice_fusion.2
  131.3 3.6 bitcast_dynamic-update-slice_fusion.2
  148.4 3.6 bitcast_dynamic-update-slice_fusion.2
  161.1 3.6 bitcast_dynamic-update-slice_fusion.2
  186.7 3.6 bitcast_dynamic-update-slice_fusion.2
  212.2 3.6 bitcast_dynamic-update-slice_fusion.2
  216.5 3.6 bitcast_dynamic-update-slice_fusion.2
  229.3 3.6 bitcast_dynamic-update-slice_fusion.2
  233.6 3.6 bitcast_dynamic-update-slice_fusion.2
  246.3 3.6 bitcast_dynamic-update-slice_fusion.2
  254.9 3.6 bitcast_dynamic-update-slice_fusion.2
  263.4 3.6 bitcast_dynamic-update-slice_fusion.2
  267.7 3.6 bitcast_dynamic-update-slice_fusion.2
  271.9 3.6 bitcast_dynamic-update-slice_fusion.2
  276.2 3.6 bitcast_dynamic-update-slice_fusion.2
  289.0 3.6 bitcast_dynamic-update-slice_fusion.2
  293.3 3.6 bitcast_dynamic-update-slice_fusion.2
  326.7 6.4 bitcast_multiply_fusion
  333.1 5.0 all-to-all-start.1
  341.4 76.6 %all-to-all-done.1 = bf16[72,192,192]{2,1,0:T(8,128)(2,1)} async-done(((bf16[72,192,192]{2,1,0:T(8,128)(2,1)}), bf16[72,192,192]{2,1,0:T(8,128)(2,1)}, u32[]{:S(2)}, u32[]{:S(2)}) %all-to-all-start.1) | async-done | bytes 5308448 | tf_op jit(solution)/shard_map/all_to_all | solution.py:107
  418.0 10.8 %fusion.33 = bf16[48,192,192]{2,0,1:T(8,128)(2,1)} fusion(bf16[72,192,192]{2,1,0:T(8,128)(2,1)} %all-to-all-done.1, s32[48]{0:T(128)S(1)} %fusion.52), kind=kOutput, calls=%fused_computation.42 | convolution fusion | flops 256583808 | bytes 8847552 | tf_op jit(solution)/shard_map/ns,sqk->nqk/dot_general | solution.py:34
  428.8 8.0 %fusion.37 = f32[48,128,128]{2,1,0:T(8,128)} fusion(bf16[48,128,192]{1,2,0:T(8,128)(2,1)} %gather_fusion.1, bf16[48,128,192]{1,2,0:T(8,128)(2,1)S(1)} %gather_fusion, bf16[48,192,192]{2,0,1:T(8,128)(2,1)} %fusion.33), kind=kOutput, calls=%fused_computation.45 | convolution fusion | flops 756154368 | bytes 11403264 | tf_op jit(solution)/shard_map/nmk,nlk->nml/dot_general | solution.py:54
  436.8 7.8 %convolution_convert_fusion.1 = bf16[48,192,192]{2,1,0:T(8,128)(2,1)} fusion(bf16[48,128,192]{1,2,0:T(8,128)(2,1)} %gather_fusion.1, bf16[48,128,192]{1,2,0:T(8,128)(2,1)S(1)} %gather_fusion, f32[48,128,128]{2,1,0:T(8,128)} %fusion.37, bf16[48,128,128]{2,1,0:T(8,128)(2,1)} %param.14, bf16[48,128,128]{2,1,0:T(8,128)(2,1)} %param.15), kind=kOutput, calls=%fused_computation.43 | convolution fusion | flops 761856000 | bytes 14548992 | tf_op jit(solution)/shard_map/nql,nlk->nqk/dot_general | solution.py:61
  444.6 6.5 convolution_convert_fusion
  451.1 4.5 copy.54
  455.6 4.8 all-to-all-start.2
  460.5 79.9 %all-to-all-done.2 = bf16[72,192,192]{2,1,0:T(8,128)(2,1)} async-done(((bf16[72,192,192]{2,1,0:T(8,128)(2,1)}), bf16[72,192,192]{2,1,0:T(8,128)(2,1)}, u32[]{:S(2)}, u32[]{:S(2)}) %all-to-all-start.2) | async-done | bytes 5308448 | tf_op jit(solution)/shard_map/all_to_all | solution.py:111
  540.4 73.1 %while.14 = (s32[]{:T(128)}, f32[6,256,256]{2,0,1:T(8,128)}, s32[9,8,4]{1,0,2:T(8,128)S(1)}, bf16[9,8,192,192]{3,2,1,0:T(8,128)(2,1)}, s32[]{:T(128)}, /*index=5*/s32[]{:T(128)}) while((s32[]{:T(128)}, f32[6,256,256]{2,0,1:T(8,128)}, s32[9,8,4]{1,0,2:T(8,128)S(1)}, bf16[9,8,192,192]{3,2,1,0:T(8,128)(2,1)}, s32[]{:T(128)}, ...), condition=%wide.region_3.4_spmd.clone.clone, body=%wide.region_2.3_spmd.clone.clone.sunk | while | flops 392039520 | bytes 8152275 | solution.py:94
  542.8 4.3 select_add_fusion.2
  549.6 5.9 select_add_fusion.2
  557.9 5.9 select_add_fusion.2
  566.2 5.9 select_add_fusion.2
  574.5 5.9 select_add_fusion.2
  582.8 5.9 select_add_fusion.2
  591.1 5.9 select_add_fusion.2
  599.4 5.9 select_add_fusion.2
  607.7 5.9 select_add_fusion.2
  616.9 34.8 %reduce-scatter.2.cloned.1.call-done = f32[1,6,64,256]{3,2,1,0:T(8,128)} async-done(((f32[1,6,256,256]{3,2,1,0:T(8,128)}), f32[1,6,64,256]{3,2,1,0:T(8,128)}) %reduce-scatter.2.cloned.1.call-update) | async-done | bytes 393232 | tf_op jit(solution)/shard_map/reduce_scatter | solution.py:113
  (260 shorter events, 252.2 us)
Async XLA Ops:
  6.5 331.5 %copy-start = (bf16[6,128,192]{1,2,0:T(8,128)(2,1)S(1)}, bf16[6,128,192]{1,2,0:T(8,128)(2,1)}, u32[]{:S(2)}) copy-start(bf16[6,128,192]{1,2,0:T(8,128)(2,1)} %param.16) | copy-start | bytes 884740
  9.8 9.9 %all-to-all-start = ((s32[8,9,4]{1,2,0:T(4,128)}), s32[8,9,4]{1,2,0:T(4,128)S(1)}, u32[]{:S(2)}, u32[]{:S(2)}) async-start(s32[8,9,4]{1,2,0:T(4,128)} %copy.48), calls=%async_computation | async-start | bytes 32768 | tf_op jit(solution)/shard_map/all_to_all | solution.py:105
  333.1 5.0 copy-start.3
  333.1 85.0 %all-to-all-start.1 = ((bf16[72,192,192]{2,1,0:T(8,128)(2,1)}), bf16[72,192,192]{2,1,0:T(8,128)(2,1)}, u32[]{:S(2)}, u32[]{:S(2)}) async-start(bf16[72,192,192]{2,1,0:T(8,128)(2,1)} %bitcast_multiply_fusion), calls=%async_computation.1 | async-start | bytes 14155776 | tf_op jit(solution)/shard_map/all_to_all | solution.py:107
  338.1 1.0 copy-start.2
  455.6 84.9 %all-to-all-start.2 = ((bf16[72,192,192]{2,1,0:T(8,128)(2,1)}), bf16[72,192,192]{2,1,0:T(8,128)(2,1)}, u32[]{:S(2)}, u32[]{:S(2)}) async-start(bf16[72,192,192]{2,1,0:T(8,128)(2,1)} %copy.54), calls=%async_computation.2 | async-start | bytes 14155776 | tf_op jit(solution)/shard_map/all_to_all | solution.py:111
  460.4 191.3 %reduce-scatter.2.cloned.1.call-start = ((), (), s32[]{:S(2)}) async-start(), calls=%async_computation.4 | async-start | bytes 1966080 | tf_op jit(solution)/shard_map/reduce_scatter | solution.py:113
  613.5 38.2 %copy-start.1 = (bf16[6,128,192]{1,2,0:T(8,128)(2,1)S(1)}, bf16[6,128,192]{1,2,0:T(8,128)(2,1)}, u32[]{:S(2)}) copy-start(bf16[6,128,192]{1,2,0:T(8,128)(2,1)} %param.16) | copy-start | bytes 884740
Sparse Core Ops, SparseCore 0:
  617.0 34.6 reduce-scatter.1
where the time goes:
time: 664 us; the launch traced here: 659 us
  local copies, waits for them, and re-layouts  319 us (48%)
  waiting for transfers between devices  196 us (30%)
  matrix products  105 us (16%)
  starting transfers between devices  15 us (2%)
  between operations  13.5 us (2%)
  other arithmetic  9.67 us (1%)
    gather x216, local copies, waits for them, and re-layouts  307 us
    all_to_all x1, waiting for transfers between devices, local(): lax.all_to_all(adjoint_slots, 'tile', split_axis=0, concat_axis=0, tiled=...  79.9 us
    all_to_all x1, waiting for transfers between devices, local(): lax.all_to_all(outgoing, 'tile', split_axis=0, concat_axis=0, tiled=True)  76.6 us
    dot_general x9, matrix products, step(): jnp.einsum('nb,npk->bpk', band_hot, placed, precision=lax.Precision.HIGHEST)  51.2 us
    reduce_scatter x1, waiting for transfers between devices, local(): lax.psum_scatter(partial_value[None], 'expo', scatter_dimension=2, tiled=...  34.8 us
    dot_general x9, matrix products, step(): jnp.einsum('npq,nqk->npk', row_hot, wide, preferred_element_type=jnp.floa...  21 us
  transfers between devices with their start and end apart: 4, of which 4 were waited for; matrix products, arithmetic and copies ran while one was open for 1% of the time, Pallas kernels for 0%

commit v1 on v0

v1 whole, which is shorter than its diff:
```python
import functools

import jax
import jax.numpy as jnp
from jax import lax
from jax.experimental import pallas as pl
from jax.experimental.pallas import tpu as pltpu
from jax.sharding import PartitionSpec as P


def slot_layout(exp_tile, exp_band, exp_offset, owners, capacity):
    target = exp_tile[:, 0]
    count = target.shape[0]
    order = jnp.arange(count, dtype=jnp.int32)
    before = (target[:, None] == target[None, :]) & (order[None, :] < order[:, None])
    rank = jnp.sum(before.astype(jnp.int32), axis=1)
    slot = target * capacity + rank
    fields = jnp.stack(
        [jnp.ones_like(target), exp_band, exp_offset[:, 0], exp_offset[:, 1], order], axis=1
    )
    slot_ids = jnp.arange(owners * capacity, dtype=jnp.int32)
    slot_hot = (slot[:, None] == slot_ids[None, :]).astype(jnp.int32)
    return jnp.sum(slot_hot[:, :, None] * fields[:, None, :], axis=0)


def compute_kernel(capacity, meta, data, model, row_wide, col_wide, row_tall, acc):
    group = pl.program_id(0)
    side = acc.shape[-1]
    reach = row_tall.shape[1] - side

    @pl.when(group == 0)
    def _():
        acc[...] = jnp.zeros_like(acc)

    def one_slot(s, carry):
        at = group * capacity + s

        @pl.when(meta[0, at] > 0)
        def _():
            band, row, col = meta[1, at], meta[2, at], meta[3, at]
            r = pltpu.roll(row_wide[band], row, 1).astype(jnp.bfloat16)
            c = pltpu.roll(col_wide[band], col, 1).astype(jnp.bfloat16)
            rt = row_tall[band, pl.ds(reach - row, side), :].astype(jnp.bfloat16)
            half = jnp.dot(r, model[band], preferred_element_type=jnp.float32).astype(jnp.bfloat16)
            predicted = lax.dot_general(
                half, c, (((1,), (1,)), ((), ())), preferred_element_type=jnp.float32
            )
            pixels = data[0, s, 0].astype(jnp.float32)
            inv_var = data[0, s, 1].astype(jnp.float32)
            weighted = (inv_var * (predicted - pixels)).astype(jnp.bfloat16)
            back = jnp.dot(rt, weighted, preferred_element_type=jnp.float32).astype(jnp.bfloat16)
            adjoint = jnp.dot(back, c, preferred_element_type=jnp.float32).astype(jnp.bfloat16)
            acc[band] += adjoint.astype(jnp.float32)

        return carry

    lax.fori_loop(0, capacity, one_slot, 0)


def local(model, exp_tile, exp_band, exp_offset, pixels, inv_var, row_op, col_op):
    owners = lax.axis_size("tile")
    count, m, _ = pixels.shape
    capacity = max(2, 3 * count // (2 * owners))
    bands, side = model.shape[1], model.shape[2]
    q = row_op.shape[2]
    reach = side - q
    requests = slot_layout(exp_tile, exp_band, exp_offset, owners, capacity)
    picked = requests[:, 4]
    outgoing = jnp.stack([pixels[picked], inv_var[picked]], axis=1)
    received = lax.all_to_all(requests, "tile", split_axis=0, concat_axis=0, tiled=True)
    arrived = lax.all_to_all(outgoing, "tile", split_axis=0, concat_axis=0, tiled=True)
    arrived = arrived.reshape(owners, capacity, 2, m, m)
    row_wide = jnp.pad(row_op.astype(jnp.float32), ((0, 0), (0, 0), (0, reach)))
    col_wide = jnp.pad(col_op.astype(jnp.float32), ((0, 0), (0, 0), (0, reach)))
    row_tall = jnp.pad(
        jnp.swapaxes(row_op.astype(jnp.float32), 1, 2), ((0, 0), (reach, reach), (0, 0))
    )
    full = lambda x: pl.BlockSpec(x.shape, lambda g, meta: (0,) * x.ndim)
    partial = pl.pallas_call(
        functools.partial(compute_kernel, capacity),
        grid_spec=pltpu.PrefetchScalarGridSpec(
            num_scalar_prefetch=1,
            grid=(owners,),
            in_specs=[
                pl.BlockSpec((1, capacity, 2, m, m), lambda g, meta: (g, 0, 0, 0, 0)),
                full(model[0]),
                full(row_wide),
                full(col_wide),
                full(row_tall),
            ],
            out_specs=pl.BlockSpec((bands, side, side), lambda g, meta: (0, 0, 0)),
        ),
        out_shape=jax.ShapeDtypeStruct((bands, side, side), jnp.float32),
        compiler_params=pltpu.CompilerParams(vmem_limit_bytes=48 * 1024 * 1024),
    )(received.T, arrived, model[0], row_wide, col_wide, row_tall)
    return lax.psum_scatter(partial[None], "expo", scatter_dimension=2, tiled=True)


def solution(mesh):
    in_specs = (
        P("tile", None, None, None),
        P(("tile", "expo"), None),
        P(("tile", "expo")),
        P(("tile", "expo"), None),
        P(("tile", "expo"), None, None),
        P(("tile", "expo"), None, None),
        P(),
        P(),
    )
    out_specs = P("tile", None, "expo", None)
    return jax.shard_map(local, mesh=mesh, in_specs=in_specs, out_specs=out_specs, check_vma=False)
```

time: 664 us -> 180 us (0.27)
  local copies, waits for them, and re-layouts: 319 us -> 10.2 us
  matrix products: 105 us -> 0 us
  waiting for transfers between devices: 196 us -> 101 us
  Pallas kernels: 0 us -> 34.6 us
    gather x218 -> x2, local copies, waits for them, and re-layouts: 310 us -> 4.88 us  [local(): outgoing = jnp.stack([pixels[picked], inv_var[picked]], axis=1)]
    dot_general x22 -> x0, matrix products: 105 us -> none  [the longest x9 51.2 us: step(): jnp.einsum('nb,npk->bpk', band_hot, placed, precision=lax.Precision.HIGHEST)]
    all_to_all x1 -> x0, waiting for transfers between devices: 79.9 us -> none  [local(): lax.all_to_all(adjoint_slots, 'tile', split_axis=0, concat_axis=0, tiled=...]
    pallas_call x0 -> x1, Pallas kernels: none -> 34.6 us  [local(): pl.pallas_call(functools.partial(compute_kernel, capacity), grid_spec=plt...]
    all_to_all x1, waiting for transfers between devices: 76.6 us -> 50.4 us  [local(): lax.all_to_all(outgoing, 'tile', split_axis=0, concat_axis=0, tiled=True)]
    reduce_scatter x1, waiting for transfers between devices: 34.8 us -> 51 us  [local(): lax.psum_scatter(partial[None], 'expo', scatter_dimension=2, tiled=True)]
  transfers between devices with their start and end apart: 4 -> 3, of which waited for: 4 -> 2; matrix products, arithmetic and copies ran while one was open for 1% -> 8% of each run, Pallas kernels for 0% -> 0%
where the time goes in v1:
time: 180 us; the launch traced here: 179 us
  waiting for transfers between devices  101 us (56%)
  Pallas kernels  34.6 us (19%)
  between operations  13.5 us (8%)
  local copies, waits for them, and re-layouts  10.2 us (6%)
  starting transfers between devices  9.94 us (6%)
  other arithmetic  9.57 us (5%)
    reduce_scatter x1, waiting for transfers between devices, local(): lax.psum_scatter(partial[None], 'expo', scatter_dimension=2, tiled=True)  51 us
    all_to_all x1, waiting for transfers between devices, local(): lax.all_to_all(outgoing, 'tile', split_axis=0, concat_axis=0, tiled=True)  50.4 us
    pallas_call x1, Pallas kernels, local(): pl.pallas_call(functools.partial(compute_kernel, capacity), grid_spec=plt...  34.6 us
    all_to_all x1, starting transfers between devices, local(): lax.all_to_all(requests, 'tile', split_axis=0, concat_axis=0, tiled=True)  5.17 us
    another operation x1, other arithmetic, local(): outgoing = jnp.stack([pixels[picked], inv_var[picked]], axis=1)  5 us
    gather x2, local copies, waits for them, and re-layouts, local(): outgoing = jnp.stack([pixels[picked], inv_var[picked]], axis=1)  4.88 us
    all_to_all x1, starting transfers between devices, local(): lax.all_to_all(outgoing, 'tile', split_axis=0, concat_axis=0, tiled=True)  4.73 us
    unnamed x12, local copies, waits for them, and re-layouts  4.34 us
  transfers between devices with their start and end apart: 3, of which 2 were waited for; matrix products, arithmetic and copies ran while one was open for 8% of the time, Pallas kernels for 0%

profile of v1, /device:TPU:0, one launch (start us, length us, event | category | flops | bytes accessed | tf_op | source)
XLA Modules:
  0.0 179.1 jit_solution(11306785772408364466)
XLA Ops:
  6.5 0.0 copy-start
  6.5 1.0 convert_reduce_fusion
  7.5 0.7 fusion.3
  8.2 0.1 fusion.1
  8.3 0.8 pad_add_fusion
  9.0 0.1 multiply_reduce_fusion
  9.1 0.1 all_to_all.11
  9.2 0.6 copy.22
  9.8 5.2 %all-to-all-start = ((s32[8,9,5]{1,2,0:T(8,128)}), s32[8,9,5]{1,2,0:T(8,128)S(1)}, u32[]{:S(2)}, u32[]{:S(2)}) async-start(s32[8,9,5]{1,2,0:T(8,128)} %copy.22), calls=%async_computation | async-start | bytes 65536 | tf_op jit(solution)/shard_map/all_to_all | solution.py:70
  15.0 0.0 copy-done
  15.0 0.0 copy-start.3
  15.1 2.4 %gather_fusion = bf16[72,128,128]{2,1,0:T(8,128)(2,1)} fusion(bf16[48,128,128]{2,1,0:T(8,128)(2,1)S(1)} %copy-done, s32[1024]{0:T(1024)S(1)} %pad_clamp_fusion), kind=kCustom, calls=%fused_computation | custom fusion | bytes 4718880 | tf_op jit(solution)/shard_map/gather | solution.py:69
  17.5 0.0 copy-done.3
  17.5 2.4 %gather_fusion.1 = bf16[72,128,128]{2,1,0:T(8,128)(2,1)} fusion(bf16[48,128,128]{2,1,0:T(8,128)(2,1)S(1)} %copy-done.3, s32[1024]{0:T(1024)S(1)} %pad_clamp_fusion), kind=kCustom, calls=%fused_computation.1 | custom fusion | bytes 4718880 | tf_op jit(solution)/shard_map/gather | solution.py:69
  19.9 5.0 %pad_maximum_fusion = bf16[72,2,128,128]{3,2,1,0:T(8,128)(2,1)} fusion(bf16[72,1,128,128]{3,2,1,0:T(8,128)(2,1)} %bitcast.26, bf16[72,1,128,128]{3,2,1,0:T(8,128)(2,1)} %bitcast.25), kind=kLoop, calls=%fused_computation.2 | loop fusion | flops 2359296 | bytes 9437184 | tf_op jit(solution)/shard_map/stack | solution.py:69
  24.9 0.0 copy-start.4
  24.9 0.0 all-to-all-done
  24.9 4.7 %all-to-all-start.1 = ((bf16[72,2,128,128]{3,2,1,0:T(8,128)(2,1)}), bf16[72,2,128,128]{3,2,1,0:T(8,128)(2,1)}, u32[]{:S(2)}, u32[]{:S(2)}) async-start(bf16[72,2,128,128]{3,2,1,0:T(8,128)(2,1)} %pad_maximum_fusion), calls=%async_computation.1 | async-start | bytes 9437184 | tf_op jit(solution)/shard_map/all_to_all | solution.py:71
  29.7 0.0 reduce-scatter.2.cloned.1.call-start
  29.7 0.0 copy-done.4
  29.7 0.2 copy.26
  29.9 0.1 pad.13.clone.row_wide
  30.1 0.1 pad.16.row_tall
  30.1 1.9 %copy.24 = bf16[6,128,192]{2,1,0:T(8,128)(2,1)} copy(bf16[6,128,192]{1,2,0:T(8,128)(2,1)} %param.15) | data formatting | bytes 589824 | tf_op args[7]
  32.0 1.9 %pad_convert_fusion.col_wide = f32[6,128,256]{2,1,0:T(8,128)} fusion(bf16[6,128,192]{2,1,0:T(8,128)(2,1)} %copy.24), kind=kLoop, calls=%fused_computation.3 | loop fusion | flops 196608 | bytes 1081344 | tf_op jit(solution)/shard_map/jit(_pad)/pad | solution.py:74
  34.0 0.1 all_to_all.13
  34.0 50.4 %all-to-all-done.1 = bf16[72,2,128,128]{3,2,1,0:T(8,128)(2,1)} async-done(((bf16[72,2,128,128]{3,2,1,0:T(8,128)(2,1)}), bf16[72,2,128,128]{3,2,1,0:T(8,128)(2,1)}, u32[]{:S(2)}, u32[]{:S(2)}) %all-to-all-start.1) | async-done | bytes 4718624 | tf_op jit(solution)/shard_map/all_to_all | solution.py:71
  84.4 0.0 copy-start.1
  84.4 1.1 copy-done.1
  85.6 0.0 copy-start.2
  85.6 1.1 copy-done.2
  86.7 34.6 %shard_map.82 = f32[6,256,256]{2,1,0:T(8,128)} custom-call(s32[5,72]{1,0:T(8,128)S(1)} %bitcast.24, bf16[8,9,2,128,128]{4,3,2,1,0:T(8,128)(2,1)} %bitcast.8.data, bf16[6,256,256]{2,1,0:T(8,128)(2,1)S(1)} %bitcast.23, f32[6,128,256]{2,1,0:T(8,128)S(1)} %pad.13.clone.row_wide, f32[6,128,256]{2,1,0:T(8,128)S(1)} %copy-done.1, f32[6,320,128]{2,1,0:T(8,128)S(1)} %pad.16.row_tall), custom_call_target="tpu_custom_call" | custom-call | tf_op jit(solution)/shard_map/pallas_call | solution.py:79
  121.3 0.0 reduce-scatter.2.cloned.1.call-update
  121.3 51.0 %reduce-scatter.2.cloned.1.call-done = f32[1,6,64,256]{3,2,1,0:T(8,128)} async-done(((f32[1,6,256,256]{3,2,1,0:T(8,128)}), f32[1,6,64,256]{3,2,1,0:T(8,128)}) %reduce-scatter.2.cloned.1.call-update) | async-done | bytes 393232 | tf_op jit(solution)/shard_map/reduce_scatter | solution.py:96
  (6 shorter events, 0.1 us)
Async XLA Ops:
  6.5 8.5 %copy-start = (bf16[48,128,128]{2,1,0:T(8,128)(2,1)S(1)}, bf16[48,128,128]{2,1,0:T(8,128)(2,1)}, u32[]{:S(2)}) copy-start(bf16[48,128,128]{2,1,0:T(8,128)(2,1)} %param.12) | copy-start | bytes 4718596
  9.8 15.1 %all-to-all-start = ((s32[8,9,5]{1,2,0:T(8,128)}), s32[8,9,5]{1,2,0:T(8,128)S(1)}, u32[]{:S(2)}, u32[]{:S(2)}) async-start(s32[8,9,5]{1,2,0:T(8,128)} %copy.22), calls=%async_computation | async-start | bytes 65536 | tf_op jit(solution)/shard_map/all_to_all | solution.py:70
  15.0 2.4 %copy-start.3 = (bf16[48,128,128]{2,1,0:T(8,128)(2,1)S(1)}, bf16[48,128,128]{2,1,0:T(8,128)(2,1)}, u32[]{:S(2)}) copy-start(bf16[48,128,128]{2,1,0:T(8,128)(2,1)} %param.13) | copy-start | bytes 4718596
  24.9 4.8 %copy-start.4 = (bf16[6,128,192]{1,2,0:T(8,128)(2,1)S(1)}, bf16[6,128,192]{1,2,0:T(8,128)(2,1)}, u32[]{:S(2)}) copy-start(bf16[6,128,192]{1,2,0:T(8,128)(2,1)} %param.14) | copy-start | bytes 884740
  24.9 59.5 %all-to-all-start.1 = ((bf16[72,2,128,128]{3,2,1,0:T(8,128)(2,1)}), bf16[72,2,128,128]{3,2,1,0:T(8,128)(2,1)}, u32[]{:S(2)}, u32[]{:S(2)}) async-start(bf16[72,2,128,128]{3,2,1,0:T(8,128)(2,1)} %pad_maximum_fusion), calls=%async_computation.1 | async-start | bytes 9437184 | tf_op jit(solution)/shard_map/all_to_all | solution.py:71
  29.7 142.6 %reduce-scatter.2.cloned.1.call-start = ((), (), s32[]{:S(2)}) async-start(), calls=%async_computation.3 | async-start | bytes 1966080 | tf_op jit(solution)/shard_map/reduce_scatter | solution.py:96
  84.4 1.1 copy-start.1
  85.6 1.1 copy-start.2
Sparse Core Ops, SparseCore 0:
  121.4 50.8 reduce-scatter.1

commit v2 on v1

v2 whole, which is shorter than its diff:
```python
import functools

import jax
import jax.numpy as jnp
from jax import lax
from jax.experimental import pallas as pl
from jax.experimental.pallas import tpu as pltpu
from jax.sharding import PartitionSpec as P

AHEAD = 4
LANES = 128
FIELDS = 8


def slot_layout(exp_tile, exp_band, exp_offset, owners):
    target = exp_tile[:, 0]
    count = target.shape[0]
    order = jnp.arange(count, dtype=jnp.int32)
    before = (target[:, None] == target[None, :]) & (order[None, :] < order[:, None])
    rank = jnp.sum(before.astype(jnp.int32), axis=1)
    zero = jnp.zeros_like(target)
    fields = jnp.stack(
        [zero + 1, exp_band, exp_offset[:, 0], exp_offset[:, 1], order, zero, zero, zero], axis=1
    )
    owner_hot = target[:, None] == jnp.arange(owners, dtype=jnp.int32)[None, :]
    slot_hot = rank[:, None] == jnp.arange(LANES, dtype=jnp.int32)[None, :]
    hot = owner_hot[:, :, None, None] & slot_hot[:, None, None, :]
    return jnp.sum(jnp.where(hot, fields[:, None, :, None], 0), axis=0)


def partner(me, step, owners):
    if owners == 8:
        third = (step + 1) // 4 - step // 4 - (step + 1) // 8 + step // 8
        fourth = step // 4 - (step + 3) // 8
        step = step + third - fourth
    out = 0
    bit = 1
    while bit < owners:
        out = out + bit * (((me // bit) % 2 + (step // bit) % 2) % 2)
        bit *= 2
    return out


def kernel(
    owners, groups, capacity,
    meta_smem, meta_out, pixels, inv_var, model, row_op, col_op,
    out,
    send, recv, meta_in, meta_s, row_wide, col_wide, row_tall, backs, cols, acc, zsend, zrecv,
    send_sem, recv_sem, msend_sem, mrecv_sem, local_sem, zsend_sem, zrecv_sem,
):
    me = lax.axis_index("tile")
    depth = lax.axis_index("expo")
    bands, side, _ = acc.shape
    m, q = row_op.shape[1:]
    reach = side - q
    rows = side // groups
    together = 3 if capacity % 3 == 0 else (2 if capacity % 2 == 0 else 1)

    barrier = pltpu.get_barrier_semaphore()

    def greet_tile(j, carry):
        pl.semaphore_signal(
            barrier, inc=1, device_id={"tile": partner(me, j, owners)},
            device_id_type=pl.DeviceIdType.MESH,
        )
        return carry

    def greet_expo(j, carry):
        pl.semaphore_signal(
            barrier, inc=1, device_id={"expo": lax.rem(depth + j, groups)},
            device_id_type=pl.DeviceIdType.MESH,
        )
        return carry

    lax.fori_loop(1, owners, greet_tile, 0)
    lax.fori_loop(1, groups, greet_expo, 0)

    def fill(j, into):
        peer = partner(me, j, owners)

        def one(s, carry):
            e = meta_smem[peer, 4, s]
            into[j, s, 0] = pixels[e]
            into[j, s, 1] = inv_var[e]
            return carry

        lax.fori_loop(0, capacity, one, 0)

    def data_copy(j):
        return pltpu.make_async_remote_copy(
            send.at[j], recv.at[j], send_sem.at[j], recv_sem.at[j],
            device_id={"tile": partner(me, j, owners)}, device_id_type=pl.DeviceIdType.MESH,
        )

    def meta_copy(j):
        peer = partner(me, j, owners)
        return pltpu.make_async_remote_copy(
            meta_out.at[peer], meta_in.at[j], msend_sem.at[j], mrecv_sem.at[j],
            device_id={"tile": peer}, device_id_type=pl.DeviceIdType.MESH,
        )

    fill(1, send)
    pl.semaphore_wait(barrier, owners + groups - 2)

    def push(j, carry):
        meta_copy(j).start()

        @pl.when(j > 1)
        def _():
            fill(j, send)

        data_copy(j).start()
        return carry

    ahead = min(AHEAD, owners - 1)
    lax.fori_loop(1, ahead + 1, push, 0)

    fill(0, recv)
    acc[...] = jnp.zeros_like(acc)
    cols[capacity] = jnp.zeros_like(cols[capacity])

    def widen(b, carry):
        zeros = jnp.zeros((m, reach), jnp.float32)
        r = jnp.concatenate([row_op[b].astype(jnp.float32), zeros], axis=1)
        row_wide[b] = r
        col_wide[b] = jnp.concatenate([col_op[b].astype(jnp.float32), zeros], axis=1)
        row_tall[b, 0:reach, :] = jnp.zeros((reach, m), jnp.float32)
        row_tall[b, reach : reach + side, :] = r.T
        return carry

    lax.fori_loop(0, bands, widen, 0)

    def compute(j):
        def some_slots(t, carry):
            slots = [t * together + u for u in range(together)]
            wide, cut = [], []
            for s in slots:
                band, row, col = meta_s[1, s], meta_s[2, s], meta_s[3, s]
                r = pltpu.roll(row_wide[band], row, 1).astype(jnp.bfloat16)
                c = pltpu.roll(col_wide[band], col, 1).astype(jnp.bfloat16)
                rt = row_tall[band, pl.ds(reach - row, side), :].astype(jnp.bfloat16)
                cols[s] = c
                wide.append((r, c, rt, band))
            halfs = [
                jnp.dot(r, model[band], preferred_element_type=jnp.float32).astype(jnp.bfloat16)
                for r, c, rt, band in wide
            ]
            predicted = [
                lax.dot_general(
                    h, w[1], (((1,), (1,)), ((), ())), preferred_element_type=jnp.float32
                )
                for h, w in zip(halfs, wide)
            ]
            weighted = [
                (
                    recv[j, s, 1].astype(jnp.float32) * (p - recv[j, s, 0].astype(jnp.float32))
                ).astype(jnp.bfloat16)
                for p, s in zip(predicted, slots)
            ]
            for w, x, s in zip(wide, weighted, slots):
                backs[s] = jnp.dot(w[2], x, preferred_element_type=jnp.float32).astype(
                    jnp.bfloat16
                )
            return carry

        lax.fori_loop(0, capacity // together, some_slots, 0)

        def one_band(b, carry):
            left = jnp.concatenate([backs[s] for s in range(capacity)], axis=1)
            right = []
            for s in range(capacity):
                mine = (meta_s[0, s] > 0) & (meta_s[1, s] == b)
                right.append(cols[jnp.where(mine, s, capacity)])
            acc[b] += jnp.dot(
                left, jnp.concatenate(right, axis=0), preferred_element_type=jnp.float32
            )
            return carry

        lax.fori_loop(0, bands, one_band, 0)

    def fetch_meta(source):
        copy = pltpu.make_async_copy(source, meta_s, local_sem)
        copy.start()
        copy.wait()

    fetch_meta(meta_out.at[me])
    compute(0)

    def turn(j, carry):
        meta_copy(j).wait_recv()
        data_copy(j).wait_recv()

        @pl.when(j + ahead < owners)
        def _():
            push(j + ahead, 0)

        fetch_meta(meta_in.at[j])
        compute(j)
        return carry

    lax.fori_loop(1, owners, turn, 0)

    def block(z):
        return pl.ds(pl.multiple_of(z * rows, rows), rows)

    def z_copy(j):
        return pltpu.make_async_remote_copy(
            zsend.at[j], zrecv.at[j], zsend_sem.at[j], zrecv_sem.at[j],
            device_id={"expo": lax.rem(depth + j, groups)}, device_id_type=pl.DeviceIdType.MESH,
        )

    def z_push(j, carry):
        zsend[j] = acc[:, block(lax.rem(depth + j, groups)), :].astype(jnp.bfloat16)
        z_copy(j).start()
        return carry

    lax.fori_loop(1, groups, z_push, 0)
    out[...] = acc[:, block(depth), :]

    def z_sum(j, carry):
        z_copy(j).wait_recv()
        out[...] += zrecv[j].astype(jnp.float32)
        return carry

    lax.fori_loop(1, groups, z_sum, 0)

    def finish(j, carry):
        meta_copy(j).wait_send()
        data_copy(j).wait_send()
        return carry

    lax.fori_loop(1, owners, finish, 0)

    def z_finish(j, carry):
        z_copy(j).wait_send()
        return carry

    lax.fori_loop(1, groups, z_finish, 0)


def local(model, exp_tile, exp_band, exp_offset, pixels, inv_var, row_op, col_op):
    owners = lax.axis_size("tile")
    groups = lax.axis_size("expo")
    count, m, _ = pixels.shape
    capacity = max(2, 3 * count // (2 * owners))
    bands, side = model.shape[1], model.shape[2]
    q = row_op.shape[2]
    reach = side - q
    rows = side // groups
    requests = slot_layout(exp_tile, exp_band, exp_offset, owners)
    vmem = pl.BlockSpec(memory_space=pltpu.VMEM)
    dma = pltpu.SemaphoreType.DMA
    result = pl.pallas_call(
        functools.partial(kernel, owners, groups, capacity),
        out_shape=jax.ShapeDtypeStruct((bands, rows, side), jnp.float32),
        in_specs=[pl.BlockSpec(memory_space=pltpu.SMEM)] + [vmem] * 6,
        out_specs=vmem,
        scratch_shapes=[
            pltpu.VMEM((owners, capacity, 2, m, m), jnp.bfloat16),
            pltpu.VMEM((owners, capacity, 2, m, m), jnp.bfloat16),
            pltpu.VMEM((owners, FIELDS, LANES), jnp.int32),
            pltpu.SMEM((FIELDS, LANES), jnp.int32),
            pltpu.VMEM((bands, m, side), jnp.float32),
            pltpu.VMEM((bands, m, side), jnp.float32),
            pltpu.VMEM((bands, reach + side, m), jnp.float32),
            pltpu.VMEM((capacity, side, m), jnp.bfloat16),
            pltpu.VMEM((capacity + 1, m, side), jnp.bfloat16),
            pltpu.VMEM((bands, side, side), jnp.float32),
            pltpu.VMEM((groups, bands, rows, side), jnp.bfloat16),
            pltpu.VMEM((groups, bands, rows, side), jnp.bfloat16),
            dma((owners,)),
            dma((owners,)),
            dma((owners,)),
            dma((owners,)),
            dma,
            dma((groups,)),
            dma((groups,)),
        ],
        compiler_params=pltpu.CompilerParams(
            collective_id=0, has_side_effects=True, vmem_limit_bytes=56 * 1024 * 1024
        ),
    )(requests, requests, pixels, inv_var, model[0], row_op, col_op)
    return result[None]


def solution(mesh):
    in_specs = (
        P("tile", None, None, None),
        P(("tile", "expo"), None),
        P(("tile", "expo")),
        P(("tile", "expo"), None),
        P(("tile", "expo"), None, None),
        P(("tile", "expo"), None, None),
        P(),
        P(),
    )
    out_specs = P("tile", None, "expo", None)
    return jax.shard_map(local, mesh=mesh, in_specs=in_specs, out_specs=out_specs, check_vma=False)
```

time: 180 us -> 92.1 us (0.51)
  the two profiles are of different devices: /device:TPU:0 before, /device:TPU:9 now
where the time goes in v2:
time: 92.1 us; the launch traced here: 91.9 us
  Pallas kernels  82.8 us (90%)
  local copies, waits for them, and re-layouts  6.33 us (7%)
  other arithmetic  2.7 us (3%)
    pallas_call x1, Pallas kernels, local(): pl.pallas_call(functools.partial(kernel, owners, groups, capacity), out_s...  82.8 us
    unnamed x3, local copies, waits for them, and re-layouts  5.53 us

profile of v2, /device:TPU:9, one launch (start us, length us, event | category | flops | bytes accessed | tf_op | source)
XLA Modules:
  0.0 91.9 jit_solution(10184025716546974406)
XLA Ops:
  0.0 0.9 convert_reduce_fusion
  0.9 0.7 stack.17
  1.7 0.1 iota_compare_fusion
  1.7 0.7 iota_compare_fusion.2
  2.5 0.1 copy.12
  2.6 0.1 broadcast_and_fusion
  2.7 0.9 select_reduce_fusion.meta_smem.meta_out
  3.5 1.9 %copy.13.row_op = bf16[6,128,192]{2,1,0:T(8,128)(2,1)} copy(bf16[6,128,192]{1,2,0:T(8,128)(2,1)} %param.14) | data formatting | bytes 589824 | tf_op args[6]
  5.4 1.9 %copy.14.col_op = bf16[6,128,192]{2,1,0:T(8,128)(2,1)} copy(bf16[6,128,192]{1,2,0:T(8,128)(2,1)} %param.15) | data formatting | bytes 589824 | tf_op args[7]
  7.3 82.8 %shard_map.85 = f32[6,64,256]{2,1,0:T(8,128)} custom-call(s32[8,8,128]{2,1,0:T(8,128)} %select_reduce_fusion.meta_smem.meta_out, s32[8,8,128]{2,1,0:T(8,128)} %select_reduce_fusion.meta_smem.meta_out, bf16[48,128,128]{2,1,0:T(8,128)(2,1)} %pixels.1, bf16[48,128,128]{2,1,0:T(8,128)(2,1)} %inv_var.1, bf16[6,256,256]{2,1,0:T(8,128)(2,1)} %bitcast.5, ...), custom_call_target="tpu_custom_call" | custom-call | tf_op jit(solution)/shard_map/pallas_call | solution.py:253
  90.1 1.8 %copy.16 = f32[1,6,64,256]{3,2,1,0:T(8,128)} copy(f32[1,6,64,256]{3,2,1,0:T(8,128)} %bitcast.4) | data formatting | bytes 786432
  (4 shorter events, 0.0 us)

commit v3 on v2

--- a/solution.py
+++ b/solution.py
@@ -7,9 +7,8 @@
 from jax.experimental.pallas import tpu as pltpu
 from jax.sharding import PartitionSpec as P
 
-AHEAD = 4
+AHEAD = 5
 LANES = 128
-FIELDS = 8
 
 
 def slot_layout(exp_tile, exp_band, exp_offset, owners):
@@ -18,14 +17,11 @@
     order = jnp.arange(count, dtype=jnp.int32)
     before = (target[:, None] == target[None, :]) & (order[None, :] < order[:, None])
     rank = jnp.sum(before.astype(jnp.int32), axis=1)
-    zero = jnp.zeros_like(target)
-    fields = jnp.stack(
-        [zero + 1, exp_band, exp_offset[:, 0], exp_offset[:, 1], order, zero, zero, zero], axis=1
-    )
+    packed = 1 + 2 * exp_band + 16 * exp_offset[:, 0] + 2048 * exp_offset[:, 1] + 262144 * order
     owner_hot = target[:, None] == jnp.arange(owners, dtype=jnp.int32)[None, :]
     slot_hot = rank[:, None] == jnp.arange(LANES, dtype=jnp.int32)[None, :]
-    hot = owner_hot[:, :, None, None] & slot_hot[:, None, None, :]
-    return jnp.sum(jnp.where(hot, fields[:, None, :, None], 0), axis=0)
+    hot = owner_hot[:, :, None] & slot_hot[:, None, :]
+    return jnp.sum(jnp.where(hot, packed[:, None, None], 0), axis=0)
 
 
 def partner(me, step, owners):
@@ -43,19 +39,34 @@
 
 def kernel(
     owners, groups, capacity,
-    meta_smem, meta_out, pixels, inv_var, model, row_op, col_op,
+    meta_smem, meta_out, pixels_hbm, inv_var_hbm, model_hbm, row_hbm, col_hbm,
     out,
+    pixels, inv_var, model, row_op, col_op, load_sem,
     send, recv, meta_in, meta_s, row_wide, col_wide, row_tall, backs, cols, acc, zsend, zrecv,
     send_sem, recv_sem, msend_sem, mrecv_sem, local_sem, zsend_sem, zrecv_sem,
 ):
     me = lax.axis_index("tile")
     depth = lax.axis_index("expo")
     bands, side, _ = acc.shape
-    m, q = row_op.shape[1:]
+    q, m = row_op.shape[1:]
     reach = side - q
     rows = side // groups
     together = 3 if capacity % 3 == 0 else (2 if capacity % 2 == 0 else 1)
 
+    loads = [
+        pltpu.make_async_copy(source, target, load_sem.at[i])
+        for i, (source, target) in enumerate(
+            (
+                (pixels_hbm, pixels),
+                (inv_var_hbm, inv_var),
+                (row_hbm, row_op),
+                (col_hbm, col_op),
+                (model_hbm, model),
+            )
+        )
+    ]
+    for load in loads:
+        load.start()
     barrier = pltpu.get_barrier_semaphore()
 
     def greet_tile(j, carry):
@@ -79,7 +90,7 @@
         peer = partner(me, j, owners)
 
         def one(s, carry):
-            e = meta_smem[peer, 4, s]
+            e = meta_smem[peer, s] // 262144
             into[j, s, 0] = pixels[e]
             into[j, s, 1] = inv_var[e]
             return carry
@@ -99,6 +110,8 @@
             device_id={"tile": peer}, device_id_type=pl.DeviceIdType.MESH,
         )
 
+    loads[0].wait()
+    loads[1].wait()
     fill(1, send)
     pl.semaphore_wait(barrier, owners + groups - 2)
 
@@ -119,13 +132,17 @@
     acc[...] = jnp.zeros_like(acc)
     cols[capacity] = jnp.zeros_like(cols[capacity])
 
+    for load in loads[2:]:
+        load.wait()
+
     def widen(b, carry):
-        zeros = jnp.zeros((m, reach), jnp.float32)
-        r = jnp.concatenate([row_op[b].astype(jnp.float32), zeros], axis=1)
-        row_wide[b] = r
-        col_wide[b] = jnp.concatenate([col_op[b].astype(jnp.float32), zeros], axis=1)
-        row_tall[b, 0:reach, :] = jnp.zeros((reach, m), jnp.float32)
-        row_tall[b, reach : reach + side, :] = r.T
+        zeros = jnp.zeros((reach, m), jnp.float32)
+        r = jnp.concatenate([row_op[b].astype(jnp.float32), zeros], axis=0)
+        c = jnp.concatenate([col_op[b].astype(jnp.float32), zeros], axis=0)
+        row_wide[b] = r.T
+        col_wide[b] = c.T
+        row_tall[b, 0:reach, :] = zeros
+        row_tall[b, reach : reach + side, :] = r
         return carry
 
     lax.fori_loop(0, bands, widen, 0)
@@ -135,7 +152,8 @@
             slots = [t * together + u for u in range(together)]
             wide, cut = [], []
             for s in slots:
-                band, row, col = meta_s[1, s], meta_s[2, s], meta_s[3, s]
+                code = meta_s[0, s]
+                band, row, col = code // 2 % 8, code // 16 % 128, code // 2048 % 128
                 r = pltpu.roll(row_wide[band], row, 1).astype(jnp.bfloat16)
                 c = pltpu.roll(col_wide[band], col, 1).astype(jnp.bfloat16)
                 rt = row_tall[band, pl.ds(reach - row, side), :].astype(jnp.bfloat16)
@@ -169,7 +187,7 @@
             left = jnp.concatenate([backs[s] for s in range(capacity)], axis=1)
             right = []
             for s in range(capacity):
-                mine = (meta_s[0, s] > 0) & (meta_s[1, s] == b)
+                mine = meta_s[0, s] % 16 == 2 * b + 1
                 right.append(cols[jnp.where(mine, s, capacity)])
             acc[b] += jnp.dot(
                 left, jnp.concatenate(right, axis=0), preferred_element_type=jnp.float32
@@ -247,19 +265,27 @@
     q = row_op.shape[2]
     reach = side - q
     rows = side // groups
-    requests = slot_layout(exp_tile, exp_band, exp_offset, owners)
+    packed = slot_layout(exp_tile, exp_band, exp_offset, owners)
+    row_tr, col_tr = jnp.swapaxes(row_op, 1, 2), jnp.swapaxes(col_op, 1, 2)
+    hbm = pl.BlockSpec(memory_space=pl.ANY)
     vmem = pl.BlockSpec(memory_space=pltpu.VMEM)
     dma = pltpu.SemaphoreType.DMA
     result = pl.pallas_call(
         functools.partial(kernel, owners, groups, capacity),
         out_shape=jax.ShapeDtypeStruct((bands, rows, side), jnp.float32),
-        in_specs=[pl.BlockSpec(memory_space=pltpu.SMEM)] + [vmem] * 6,
+        in_specs=[pl.BlockSpec(memory_space=pltpu.SMEM), vmem] + [hbm] * 5,
         out_specs=vmem,
         scratch_shapes=[
+            pltpu.VMEM(pixels.shape, pixels.dtype),
+            pltpu.VMEM(inv_var.shape, inv_var.dtype),
+            pltpu.VMEM(model.shape[1:], model.dtype),
+            pltpu.VMEM(row_tr.shape, row_tr.dtype),
+            pltpu.VMEM(col_tr.shape, col_tr.dtype),
+            dma((5,)),
             pltpu.VMEM((owners, capacity, 2, m, m), jnp.bfloat16),
             pltpu.VMEM((owners, capacity, 2, m, m), jnp.bfloat16),
-            pltpu.VMEM((owners, FIELDS, LANES), jnp.int32),
-            pltpu.SMEM((FIELDS, LANES), jnp.int32),
+            pltpu.VMEM((owners, 1, LANES), jnp.int32),
+            pltpu.SMEM((1, LANES), jnp.int32),
             pltpu.VMEM((bands, m, side), jnp.float32),
             pltpu.VMEM((bands, m, side), jnp.float32),
             pltpu.VMEM((bands, reach + side, m), jnp.float32),
@@ -279,7 +305,7 @@
         compiler_params=pltpu.CompilerParams(
             collective_id=0, has_side_effects=True, vmem_limit_bytes=56 * 1024 * 1024
         ),
-    )(requests, requests, pixels, inv_var, model[0], row_op, col_op)
+    )(packed, packed[:, None, :], pixels, inv_var, model[0], row_tr, col_tr)
     return result[None]
 
 

time: 92.1 us -> 87.1 us (0.946)
  local copies, waits for them, and re-layouts: 6.33 us -> 1.78 us
  Pallas kernels: 82.8 us -> 81.8 us
    unnamed x3 -> x1, local copies, waits for them, and re-layouts: 5.53 us -> 1.78 us
    pallas_call x1, Pallas kernels: 82.8 us -> 81.8 us  [local(): pl.pallas_call(functools.partial(kernel, owners, groups, capacity), out_s...]
where the time goes in v3:
time: 87.1 us; the launch traced here: 86.9 us
  Pallas kernels  81.8 us (94%)
  other arithmetic  3.25 us (4%)
  local copies, waits for them, and re-layouts  1.78 us (2%)
    pallas_call x1, Pallas kernels, local(): pl.pallas_call(functools.partial(kernel, owners, groups, capacity), out_s...  81.8 us
    unnamed x1, local copies, waits for them, and re-layouts  1.78 us

profile of v3, /device:TPU:9, one launch (start us, length us, event | category | flops | bytes accessed | tf_op | source)
XLA Modules:
  0.0 86.9 jit_solution(16829893615509313615)
XLA Ops:
  0.0 0.9 %convert_reduce_fusion = s32[48]{0:T(128)S(1)} fusion(s32[48]{0:T(128)} %bitcast.19), kind=kLoop, calls=%fused_computation.2 | loop fusion | flops 11472 | bytes 384 | tf_op jit(solution)/shard_map/reduce_sum | solution.py:19
  0.9 0.8 fusion.1
  1.7 0.1 iota_compare_fusion
  1.8 0.7 iota_compare_fusion.2
  2.5 0.8 select_reduce_fusion.meta_smem
  3.3 81.8 %shard_map.85 = f32[6,64,256]{2,1,0:T(8,128)} custom-call(s32[8,128]{1,0:T(8,128)} %select_reduce_fusion.meta_smem, s32[8,1,128]{2,1,0:T(1,128)} %bitcast.18, bf16[48,128,128]{2,1,0:T(8,128)(2,1)} %pixels_hbm.1, bf16[48,128,128]{2,1,0:T(8,128)(2,1)} %inv_var_hbm.1, bf16[6,256,256]{2,1,0:T(8,128)(2,1)} %bitcast.15, bf16[6,192,128]{2,1,0:T(8,128)(2,1)} %bitcast.16, ...), custom_call_target="tpu_custom_call" | custom-call | tf_op jit(solution)/shard_map/pallas_call | solution.py:273
  85.1 1.8 %copy.10 = f32[1,6,64,256]{3,2,1,0:T(8,128)} copy(f32[1,6,64,256]{3,2,1,0:T(8,128)} %bitcast.14) | data formatting | bytes 786432

commit v4 on v3

--- a/solution.py
+++ b/solution.py
@@ -7,7 +7,7 @@
 from jax.experimental.pallas import tpu as pltpu
 from jax.sharding import PartitionSpec as P
 
-AHEAD = 5
+AHEAD = 6
 LANES = 128
 
 
@@ -115,9 +115,13 @@
     fill(1, send)
     pl.semaphore_wait(barrier, owners + groups - 2)
 
+    def push_meta(j, carry):
+        meta_copy(j).start()
+        return carry
+
+    lax.fori_loop(1, owners, push_meta, 0)
+
     def push(j, carry):
-        meta_copy(j).start()
-
         @pl.when(j > 1)
         def _():
             fill(j, send)
@@ -147,12 +151,29 @@
 
     lax.fori_loop(0, bands, widen, 0)
 
+    def block(z):
+        return pl.ds(pl.multiple_of(z * rows, rows), rows)
+
+    def z_copy(j, b):
+        return pltpu.make_async_remote_copy(
+            zsend.at[j, b], zrecv.at[j, b], zsend_sem.at[j, b], zrecv_sem.at[j, b],
+            device_id={"expo": lax.rem(depth + j, groups)}, device_id_type=pl.DeviceIdType.MESH,
+        )
+
+    def z_push(b):
+        def one(j, carry):
+            zsend[j, b] = acc[b, block(lax.rem(depth + j, groups)), :].astype(jnp.bfloat16)
+            z_copy(j, b).start()
+            return carry
+
+        lax.fori_loop(1, groups, one, 0)
+
     def compute(j):
         def some_slots(t, carry):
             slots = [t * together + u for u in range(together)]
             wide, cut = [], []
             for s in slots:
-                code = meta_s[0, s]
+                code = meta_s[j, 0, s]
                 band, row, col = code // 2 % 8, code // 16 % 128, code // 2048 % 128
                 r = pltpu.roll(row_wide[band], row, 1).astype(jnp.bfloat16)
                 c = pltpu.roll(col_wide[band], col, 1).astype(jnp.bfloat16)
@@ -187,60 +208,56 @@
             left = jnp.concatenate([backs[s] for s in range(capacity)], axis=1)
             right = []
             for s in range(capacity):
-                mine = meta_s[0, s] % 16 == 2 * b + 1
+                mine = meta_s[j, 0, s] % 16 == 2 * b + 1
                 right.append(cols[jnp.where(mine, s, capacity)])
             acc[b] += jnp.dot(
                 left, jnp.concatenate(right, axis=0), preferred_element_type=jnp.float32
             )
+
+            @pl.when(j == owners - 1)
+            def _():
+                z_push(b)
+
             return carry
 
         lax.fori_loop(0, bands, one_band, 0)
 
-    def fetch_meta(source):
-        copy = pltpu.make_async_copy(source, meta_s, local_sem)
+    def fetch_meta(j, source):
+        copy = pltpu.make_async_copy(source, meta_s.at[j], local_sem)
         copy.start()
         copy.wait()
 
-    fetch_meta(meta_out.at[me])
-    compute(0)
+    fetch_meta(0, meta_out.at[me])
+    compute(jnp.int32(0))
+
+    def arrive(j, carry):
+        meta_copy(j).wait_recv()
+        fetch_meta(j, meta_in.at[j])
+        return carry
+
+    lax.fori_loop(1, owners, arrive, 0)
 
     def turn(j, carry):
-        meta_copy(j).wait_recv()
         data_copy(j).wait_recv()
 
         @pl.when(j + ahead < owners)
         def _():
             push(j + ahead, 0)
 
-        fetch_meta(meta_in.at[j])
         compute(j)
         return carry
 
     lax.fori_loop(1, owners, turn, 0)
 
-    def block(z):
-        return pl.ds(pl.multiple_of(z * rows, rows), rows)
-
-    def z_copy(j):
-        return pltpu.make_async_remote_copy(
-            zsend.at[j], zrecv.at[j], zsend_sem.at[j], zrecv_sem.at[j],
-            device_id={"expo": lax.rem(depth + j, groups)}, device_id_type=pl.DeviceIdType.MESH,
-        )
-
-    def z_push(j, carry):
-        zsend[j] = acc[:, block(lax.rem(depth + j, groups)), :].astype(jnp.bfloat16)
-        z_copy(j).start()
-        return carry
-
-    lax.fori_loop(1, groups, z_push, 0)
     out[...] = acc[:, block(depth), :]
 
     def z_sum(j, carry):
-        z_copy(j).wait_recv()
-        out[...] += zrecv[j].astype(jnp.float32)
-        return carry
-
-    lax.fori_loop(1, groups, z_sum, 0)
+        b, peer = j // (groups - 1), j % (groups - 1) + 1
+        z_copy(peer, b).wait_recv()
+        out[b] += zrecv[peer, b].astype(jnp.float32)
+        return carry
+
+    lax.fori_loop(0, bands * (groups - 1), z_sum, 0)
 
     def finish(j, carry):
         meta_copy(j).wait_send()
@@ -250,10 +267,10 @@
     lax.fori_loop(1, owners, finish, 0)
 
     def z_finish(j, carry):
-        z_copy(j).wait_send()
-        return carry
-
-    lax.fori_loop(1, groups, z_finish, 0)
+        z_copy(j % (groups - 1) + 1, j // (groups - 1)).wait_send()
+        return carry
+
+    lax.fori_loop(0, bands * (groups - 1), z_finish, 0)
 
 
 def local(model, exp_tile, exp_band, exp_offset, pixels, inv_var, row_op, col_op):
@@ -285,7 +302,7 @@
             pltpu.VMEM((owners, capacity, 2, m, m), jnp.bfloat16),
             pltpu.VMEM((owners, capacity, 2, m, m), jnp.bfloat16),
             pltpu.VMEM((owners, 1, LANES), jnp.int32),
-            pltpu.SMEM((1, LANES), jnp.int32),
+            pltpu.SMEM((owners, 1, LANES), jnp.int32),
             pltpu.VMEM((bands, m, side), jnp.float32),
             pltpu.VMEM((bands, m, side), jnp.float32),
             pltpu.VMEM((bands, reach + side, m), jnp.float32),
@@ -299,8 +316,8 @@
             dma((owners,)),
             dma((owners,)),
             dma,
-            dma((groups,)),
-            dma((groups,)),
+            dma((groups, bands)),
+            dma((groups, bands)),
         ],
         compiler_params=pltpu.CompilerParams(
             collective_id=0, has_side_effects=True, vmem_limit_bytes=56 * 1024 * 1024

time: 87.1 us -> 87.4 us (level)
  the two profiles are of different devices: /device:TPU:9 before, /device:TPU:0 now
where the time goes in v4:
time: 87.4 us; the launch traced here: 87.1 us
  Pallas kernels  82.1 us (94%)
  other arithmetic  3.25 us (4%)
  local copies, waits for them, and re-layouts  1.78 us (2%)
    pallas_call x1, Pallas kernels, local(): pl.pallas_call(functools.partial(kernel, owners, groups, capacity), out_s...  82.1 us
    unnamed x1, local copies, waits for them, and re-layouts  1.78 us

profile of v4, /device:TPU:0, one launch (start us, length us, event | category | flops | bytes accessed | tf_op | source)
XLA Modules:
  0.0 87.1 jit_solution(5553562434004429399)
XLA Ops:
  0.0 0.9 %convert_reduce_fusion = s32[48]{0:T(128)S(1)} fusion(s32[48]{0:T(128)} %bitcast.19), kind=kLoop, calls=%fused_computation.2 | loop fusion | flops 11472 | bytes 384 | tf_op jit(solution)/shard_map/reduce_sum | solution.py:19
  0.9 0.8 fusion.1
  1.7 0.1 iota_compare_fusion
  1.8 0.7 iota_compare_fusion.2
  2.5 0.8 select_reduce_fusion.meta_smem
  3.3 82.1 %shard_map.85 = f32[6,64,256]{2,1,0:T(8,128)} custom-call(s32[8,128]{1,0:T(8,128)} %select_reduce_fusion.meta_smem, s32[8,1,128]{2,1,0:T(1,128)} %bitcast.18, bf16[48,128,128]{2,1,0:T(8,128)(2,1)} %pixels_hbm.1, bf16[48,128,128]{2,1,0:T(8,128)(2,1)} %inv_var_hbm.1, bf16[6,256,256]{2,1,0:T(8,128)(2,1)} %bitcast.15, bf16[6,192,128]{2,1,0:T(8,128)(2,1)} %bitcast.16, ...), custom_call_target="tpu_custom_call" | custom-call | tf_op jit(solution)/shard_map/pallas_call | solution.py:290
  85.4 1.8 %copy.10 = f32[1,6,64,256]{3,2,1,0:T(8,128)} copy(f32[1,6,64,256]{3,2,1,0:T(8,128)} %bitcast.14) | data formatting | bytes 786432
